TPU v7x, 256 devices: a whole 4x4x8 slice. The times are simulated.
256 devices in a mesh: row: 16 (over z, core), col: 16 (over y, x).
Axes of the slice: x: 4, y: 4, z: 8, core: 2. Of those that a mesh axis runs over, the one named last changes fastest.
Arguments:
- tokens: bfloat16 [1024, 12288], P('col', 'row'), may hold values from -120 to 120, as said below
- norm_gain: float32 [12288], P('row'), may hold values from 0.1 to 1.9
- norm_bias: float32 [12288], P('row'), may hold values from -3 to 3
- weight_in: bfloat16 [12288, 49152], P('row', 'col'), may hold values from -0.0546875 to 0.0546875
- bias_in: float32 [49152], P('col'), may hold values from -3 to 3
- weight_out: bfloat16 [49152, 12288], P('col', 'row'), may hold values from -0.02734375 to 0.02734375
- bias_out: float32 [12288], P('row'), may hold values from -3 to 3
Outputs:
- block_out: bfloat16 [1024, 12288], P('col', 'row')
Inputs may be any that keep to these rules, and one draw needn't show every extreme that they name: `tokens`: real-valued activations.
All inputs are finite; a program needn't handle non-finite values.
Results may differ from a plain program's by a relative error of at most 0.0075.
Values may be sent and summed in bfloat16 or wider, within the bound.
No kernel may reach another device: no remote copies, remote signals or barrier semaphores. Data moves between devices by JAX's collectives and lax.ppermute only.
A program may use at most 64 MiB of HBM per device.

v0:
```python
import jax
import jax.numpy as jnp
from jax import lax
from jax.sharding import PartitionSpec as P

epsilon = 1e-05


def body(tokens, norm_gain, norm_bias, weight_in, bias_in, weight_out, bias_out):
    floats = tokens.astype(jnp.float32)
    features_all = lax.axis_size("row") * floats.shape[1]
    sums_one = lax.psum(jnp.sum(floats, axis=1), "row")
    center = sums_one / features_all
    differ = floats - center[:, None]
    variance = lax.psum(jnp.sum(differ * differ, axis=1), "row") / features_all
    normed = (differ * lax.rsqrt(variance + epsilon)[:, None] * norm_gain + norm_bias).astype(
        jnp.bfloat16
    )
    gathered = lax.all_gather(normed, "col", axis=0, tiled=True)
    preact = lax.psum_scatter(
        jnp.dot(gathered, weight_in, preferred_element_type=jnp.float32).astype(jnp.bfloat16),
        "row",
        scatter_dimension=0,
        tiled=True,
    ).astype(jnp.float32)
    hidden = jax.nn.gelu(preact + bias_in, approximate=True).astype(jnp.bfloat16)
    partial_value = jnp.dot(
        lax.all_gather(hidden, "row", axis=0, tiled=True),
        weight_out,
        preferred_element_type=jnp.float32,
    )
    summed = lax.psum_scatter(
        partial_value.astype(jnp.bfloat16), "col", scatter_dimension=0, tiled=True
    ).astype(jnp.float32)
    return (summed + bias_out + floats).astype(jnp.bfloat16)


def solution(mesh):
    placed = (
        P("col", "row"),
        P("row"),
        P("row"),
        P("row", "col"),
        P("col"),
        P("col", "row"),
        P("row"),
    )
    return jax.shard_map(
        body, mesh=mesh, in_specs=placed, out_specs=P("col", "row"), check_vma=False
    )
```

profile of v0, /device:TPU:1, one launch (start us, length us, event | category | flops | bytes accessed | tf_op | source)
XLA Modules:
  0.0 325.8 jit_solution(7002825830133349916)
XLA Ops:
  6.5 0.0 all-gather.3.cloned.1.call-start
  6.5 1.0 convert_reduce_fusion
  7.5 27.4 %psum.14 = f32[64]{0:T(128)S(1)} all-reduce(f32[64]{0:T(128)S(1)} %convert_reduce_fusion), channel_id=1, replica_groups=mesh['row'=16,'col'=16] {'row'}, use_global_device_ids=true, to_apply=%region_1.0 | all-reduce | flops 64 | bytes 512 | tf_op jit(solution)/shard_map/psum | solution.py:12
  35.0 1.1 fusion.10
  36.1 25.8 %psum.15 = f32[64]{0:T(128)S(1)} all-reduce(f32[64]{0:T(128)S(1)} %fusion.10), channel_id=1, replica_groups=mesh['row'=16,'col'=16] {'row'}, use_global_device_ids=true, to_apply=%region_3.0 | all-reduce | flops 64 | bytes 512 | tf_op jit(solution)/shard_map/psum | solution.py:15
  61.9 1.7 fusion.13
  63.5 0.0 all-gather.3.cloned.1.call-update
  63.6 0.0 reduce-scatter.3.cloned.1.call-start
  63.6 45.8 %all-gather.3.cloned.1.call-done = bf16[1024,768]{1,0:T(8,128)(2,1)} async-done(((bf16[64,768]{1,0:T(8,128)(2,1)}), bf16[1024,768]{1,0:T(8,128)(2,1)}) %all-gather.3.cloned.1.call-update) | async-done | bytes 1572880 | tf_op jit(solution)/shard_map/all_gather | solution.py:19
  109.4 9.1 %convolution_convert_fusion = bf16[1024,3072]{1,0:T(8,128)(2,1)} fusion(bf16[1024,768]{1,0:T(8,128)(2,1)} %all-gather.3.cloned.1.call-done, bf16[768,3072]{1,0:T(8,128)(2,1)} %param.10), kind=kOutput, calls=%fused_computation | convolution fusion | flops 4834983936 | bytes 12582912 | tf_op jit(solution)/shard_map/dot_general | solution.py:21
  118.5 0.0 copy-start.1
  118.5 0.0 reduce-scatter.3.cloned.1.call-update
  118.5 0.0 all-gather.5.cloned.1.call-start
  118.5 64.0 %reduce-scatter.3.cloned.1.call-done = bf16[64,3072]{1,0:T(8,128)(2,1)} async-done(((bf16[1024,3072]{1,0:T(8,128)(2,1)}), bf16[64,3072]{1,0:T(8,128)(2,1)}) %reduce-scatter.3.cloned.1.call-update) | async-done | bytes 393232 | tf_op jit(solution)/shard_map/reduce_scatter | solution.py:20
  182.5 0.0 copy-done.1
  182.5 2.0 fusion.7
  184.5 0.0 all-gather.5.cloned.1.call-update
  184.6 0.0 copy-start
  184.6 0.0 copy-start.2
  184.6 0.0 reduce-scatter.5.cloned.1.call-start
  184.6 48.3 %all-gather.5.cloned.1.call-done = bf16[1024,3072]{1,0:T(8,128)(2,1)} async-done(((bf16[64,3072]{1,0:T(8,128)(2,1)}), bf16[1024,3072]{1,0:T(8,128)(2,1)}) %all-gather.5.cloned.1.call-update) | async-done | bytes 6291472 | tf_op jit(solution)/shard_map/all_gather | solution.py:28
  232.9 9.4 %convolution_convert_fusion.1 = bf16[1024,768]{1,0:T(8,128)(2,1)} fusion(bf16[1024,3072]{1,0:T(8,128)(2,1)} %all-gather.5.cloned.1.call-done, bf16[3072,768]{1,0:T(8,128)(2,1)} %param.12), kind=kOutput, calls=%fused_computation.1 | convolution fusion | flops 4832624640 | bytes 12582912 | tf_op jit(solution)/shard_map/dot_general | solution.py:27
  242.3 0.0 reduce-scatter.5.cloned.1.call-update
  242.3 75.4 %reduce-scatter.5.cloned.1.call-done = bf16[64,768]{1,0:T(8,128)(2,1)} async-done(((bf16[1024,768]{1,0:T(8,128)(2,1)}), bf16[64,768]{1,0:T(8,128)(2,1)}) %reduce-scatter.5.cloned.1.call-update) | async-done | bytes 98320 | tf_op jit(solution)/shard_map/reduce_scatter | solution.py:32
  317.7 0.0 copy-done
  317.7 0.0 copy-done.2
  317.7 1.6 fusion.14
  (2 shorter events, 0.0 us)
Async XLA Ops:
  6.5 102.9 %all-gather.3.cloned.1.call-start = ((), (), s32[]{:S(2)}) async-start(), calls=%async_computation.2 | async-start | bytes 1671168 | tf_op jit(solution)/shard_map/all_gather | solution.py:19
  63.6 118.9 %reduce-scatter.3.cloned.1.call-start = ((), (), s32[]{:S(2)}) async-start(), calls=%async_computation.3 | async-start | bytes 6684672 | tf_op jit(solution)/shard_map/reduce_scatter | solution.py:20
  118.5 64.0 %copy-start.1 = (f32[3072]{0:T(1024)S(1)}, f32[3072]{0:T(1024)}, u32[]{:S(2)}) copy-start(f32[3072]{0:T(1024)} %param.11) | copy-start | bytes 36868
  118.5 114.4 %all-gather.5.cloned.1.call-start = ((), (), s32[]{:S(2)}) async-start(), calls=%async_computation.4 | async-start | bytes 6684672 | tf_op jit(solution)/shard_map/all_gather | solution.py:28
  184.6 133.1 %copy-start = (bf16[64,768]{1,0:T(8,128)(2,1)S(1)}, bf16[64,768]{1,0:T(8,128)(2,1)}, u32[]{:S(2)}) copy-start(bf16[64,768]{1,0:T(8,128)(2,1)} %param.7) | copy-start | bytes 294916
  184.6 133.1 %copy-start.2 = (f32[768]{0:T(1024)S(1)}, f32[768]{0:T(1024)}, u32[]{:S(2)}) copy-start(f32[768]{0:T(1024)} %param.13) | copy-start | bytes 9220
  184.6 133.1 %reduce-scatter.5.cloned.1.call-start = ((), (), s32[]{:S(2)}) async-start(), calls=%async_computation.5 | async-start | bytes 1671168 | tf_op jit(solution)/shard_map/reduce_scatter | solution.py:32
Sparse Core Ops, SparseCore 0:
  63.7 45.6 all-gather.2
  118.6 63.8 reduce-scatter.2
  184.7 48.1 all-gather.4
  242.4 75.2 reduce-scatter.4
where the time goes:
time: 326 us
  waiting for transfers between devices  233 us (71%)
  blocking collectives  53.2 us (16%)
  matrix products  18.4 us (6%)
  between operations  13.2 us (4%)
  other arithmetic  7.37 us (2%)
    reduce_scatter x1, waiting for transfers between devices, body(): lax.psum_scatter(partial_value.astype(jnp.bfloat16), 'col', scatter_dimen...  75.4 us
    reduce_scatter x1, waiting for transfers between devices, body(): lax.psum_scatter(jnp.dot(gathered, weight_in, preferred_element_type=jnp....  64 us
    all_gather x1, waiting for transfers between devices, body(): lax.all_gather(hidden, 'row', axis=0, tiled=True)  48.3 us
    all_gather x1, waiting for transfers between devices, body(): gathered = lax.all_gather(normed, 'col', axis=0, tiled=True)  45.8 us
    psum x1, blocking collectives, body(): sums_one = lax.psum(jnp.sum(floats, axis=1), 'row')  27.4 us
    psum x1, blocking collectives, body(): variance = lax.psum(jnp.sum(differ * differ, axis=1), 'row') / features_all  25.8 us
    dot_general x1, matrix products, body(): jnp.dot(lax.all_gather(hidden, 'row', axis=0, tiled=True), weight_out, pr...  9.38 us
    dot_general x1, matrix products, body(): jnp.dot(gathered, weight_in, preferred_element_type=jnp.float32)  9.05 us
  transfers between devices with their start and end apart: 4, of which 4 were waited for; matrix products, arithmetic and copies ran while one was open for 0% of the time, Pallas kernels for 0%

commit v1 on v0

v1 whole, which is shorter than its diff:
```python
import jax
import jax.numpy as jnp
from jax import lax
from jax.experimental import pallas as pl
from jax.experimental.pallas import tpu as pltpu
from jax.sharding import Mesh
from jax.sharding import PartitionSpec as P

epsilon = 1e-05
planes = 8
parts = 2
plane = ("y", "x")
megabyte = 2**20


def swap(value):
    return lax.ppermute(value, "core", [(0, 1), (1, 0)])


def onward(value, distance=1):
    pairs = []
    for z in range(planes):
        pairs.append((2 * z, 2 * ((z + distance) % planes)))
        pairs.append((2 * z + 1, 2 * ((z - distance) % planes) + 1))
    return lax.ppermute(value, ("z", "core"), pairs)


def add(*terms):
    total = terms[0].astype(jnp.float32)
    for term in terms[1:]:
        total = total + term.astype(jnp.float32)
    return total


def low(*terms):
    return add(*terms).astype(jnp.bfloat16)


def gather_tops(tops):
    pair = jnp.stack([tops, swap(tops)])
    near = [onward(pair, distance) for distance in (1, 2, 3)]
    near.append(onward(tops, 4)[None])
    near = jnp.concatenate(near)
    return pair, near, swap(near)


def block_index(z, steps, which):
    return 2 * lax.rem(z + steps + planes, planes) + which


def near_and_far(z, core):
    way = 1 - 2 * core
    out = [(0, core), (0, 1 - core)]
    for steps in (1, 2, 3):
        out += [(-way * steps, core), (-way * steps, 1 - core)]
    out.append((4, core))
    for steps in (1, 2, 3):
        out += [(way * steps, 1 - core), (way * steps, core)]
    out.append((4, 1 - core))
    return [block_index(z, steps, which) for steps, which in out]


def first_kernel(place, gathered, gain, weight, *refs):
    theirs, ours, left, notes = refs[-4:]
    z, core = place[0], place[1]
    rows, features = gathered.shape[1:]
    way = 1 - 2 * core

    @pl.when(pl.program_id(0) == 0)
    def _():
        wanted = [block_index(z, 4, 1 - core)]
        for steps in (3, 2, 1):
            wanted.append(block_index(z, -way * steps, 1 - core))
            wanted.append(block_index(z, -way * steps, core))
        wanted.append(block_index(z, 4, core))
        for steps in (3, 2, 1, 0):
            wanted.append(block_index(z, way * steps, core))
            wanted.append(block_index(z, way * steps, 1 - core))
        lane = lax.broadcasted_iota(jnp.int32, (rows, 128), 1)
        kind = lax.div(lane, 16)
        here = lane - 16 * kind == 2 * z + core
        for slot, number in enumerate(wanted):
            span = slice(slot * rows, (slot + 1) * rows)
            block = gathered[number].astype(jnp.float32)
            mean = jnp.sum(block, axis=1, keepdims=True) / features
            differ = block - mean
            left[span] = (differ * gain[...]).astype(jnp.bfloat16)
            note = jnp.zeros((rows, 128), jnp.float32)
            squares = jnp.sum(differ * differ, axis=1, keepdims=True)
            for base, value in ((0, mean), (3, squares)):
                rest = jnp.broadcast_to(value, (rows, 128))
                for piece in range(3):
                    part = rest.astype(jnp.bfloat16).astype(jnp.float32)
                    note = jnp.where(kind == base + piece, part, note)
                    rest = rest - part
            notes[span] = jnp.where(here, note, 0.0).astype(jnp.bfloat16)

    value = jnp.dot(left[...], weight[...], preferred_element_type=jnp.float32)
    theirs[...] = value[: 7 * rows].astype(jnp.bfloat16)
    ours[...] = value[7 * rows :].astype(jnp.bfloat16)

    @pl.when(pl.program_id(0) == pl.num_programs(0) - 1)
    def _():
        theirs[:, -128:] = notes[: 7 * rows]
        ours[:, -128:] = notes[7 * rows :]


def first_product(place, gathered, part, gain, weight, *before):
    blocks, features = gathered.shape[0], gathered.shape[2]
    rows = gathered.shape[1] // parts
    units, step = weight.shape[1], 640
    return pl.pallas_call(
        first_kernel,
        grid=((units + 128) // step,),
        in_specs=[
            pl.BlockSpec(memory_space=pltpu.SMEM),
            pl.BlockSpec((blocks, rows, features), lambda i: (0, part, 0)),
            pl.BlockSpec((1, features), lambda i: (0, 0)),
            pl.BlockSpec((features, step), lambda i: (0, i)),
        ]
        + [pl.BlockSpec(memory_space=pl.ANY)] * len(before),
        out_specs=[
            pl.BlockSpec((7 * rows, step), lambda i: (0, i)),
            pl.BlockSpec((9 * rows, step), lambda i: (0, i)),
        ],
        out_shape=[
            jax.ShapeDtypeStruct((7 * rows, units + 128), jnp.bfloat16),
            jax.ShapeDtypeStruct((9 * rows, units + 128), jnp.bfloat16),
        ],
        scratch_shapes=[
            pltpu.VMEM((blocks * rows, features), jnp.bfloat16),
            pltpu.VMEM((blocks * rows, 128), jnp.bfloat16),
        ],
        compiler_params=pltpu.CompilerParams(vmem_limit_bytes=24 * megabyte),
        cost_estimate=pl.CostEstimate(
            flops=2 * blocks * rows * features * units,
            bytes_accessed=2 * (features * units + blocks * rows * (features + units)),
            transcendentals=0,
        ),
    )(place, gathered, gain.reshape(1, features), weight, *before)


def activate_kernel(place, ours, moving, other, pair, near, far, bias, *refs):
    out = refs[-1]
    z, core = place[0], place[1]
    rows, units = out.shape
    features = 768
    total = ours[...].astype(jnp.float32) + moving[...].astype(jnp.float32)
    total = total + other[...].astype(jnp.float32)
    notes, total = total[:, units:], total[:, :units]
    lane = lax.broadcasted_iota(jnp.int32, (rows, 128), 1)
    kind = lax.div(lane, 16)
    lane = lane - 16 * kind
    tops = [pair[0], pair[1]] + [near[i] for i in range(7)] + [far[i] for i in range(7)]
    means, squares = [], 0.0
    for number in near_and_far(z, core):
        mine = jnp.where(lane == number, notes, 0.0)
        means.append(jnp.sum(jnp.where(kind < 3, mine, 0.0), axis=1, keepdims=True))
        squares = squares + jnp.sum(jnp.where(kind >= 3, mine, 0.0), axis=1, keepdims=True)
    center = sum(means) / len(means)
    moved, biases = 0.0, bias[...]
    for mean, top in zip(means, tops):
        away = mean - center
        squares = squares + features * away * away
        moved = moved + away * top[0:1]
        biases = biases + top[1:2]
    scale = lax.rsqrt(squares / (len(means) * features) + epsilon)
    preact = (total + moved) * scale + biases
    out[...] = jax.nn.gelu(preact, approximate=True).astype(jnp.bfloat16)


def activate(place, ours, moving, other, tops, bias, *before):
    rows, wide = other.shape
    units = bias.shape[0]
    tops_specs = [pl.BlockSpec(top.shape, lambda i: (0, 0, 0)) for top in tops]
    return pl.pallas_call(
        activate_kernel,
        grid=(1,),
        in_specs=[
            pl.BlockSpec(memory_space=pltpu.SMEM),
            pl.BlockSpec((rows, wide), lambda i: (7, 0)),
            pl.BlockSpec((rows, wide), lambda i: (0, 0)),
            pl.BlockSpec((rows, wide), lambda i: (0, 0)),
        ]
        + tops_specs
        + [pl.BlockSpec((1, units), lambda i: (0, 0))]
        + [pl.BlockSpec(memory_space=pl.ANY)] * len(before),
        out_specs=pl.BlockSpec((rows, units), lambda i: (0, 0)),
        out_shape=jax.ShapeDtypeStruct((rows, units), jnp.bfloat16),
        compiler_params=pltpu.CompilerParams(vmem_limit_bytes=24 * megabyte),
        cost_estimate=pl.CostEstimate(
            flops=60 * rows * units, bytes_accessed=12 * rows * units, transcendentals=rows * units
        ),
    )(place, ours, moving, other, *tops, bias.reshape(1, units), *before)


def tops_kernel(gain, bias, weight, *refs):
    out = refs[-1]
    rows = []
    for value in (gain[...], bias[...]):
        for _ in range(3):
            piece = value.astype(jnp.bfloat16).astype(jnp.float32)
            rows.append(piece)
            value = value - piece
    rows += [jnp.zeros_like(rows[0])] * 10
    left = jnp.concatenate(rows).astype(jnp.bfloat16)
    value = jnp.dot(left, weight[...], preferred_element_type=jnp.float32)
    out[0:1] = value[0:1] + value[1:2] + value[2:3]
    out[1:2] = value[3:4] + value[4:5] + value[5:6]


def tops_product(gain, bias, weight, *before):
    features, units = weight.shape
    step = 512
    return pl.pallas_call(
        tops_kernel,
        grid=(units // step,),
        in_specs=[pl.BlockSpec((1, features), lambda i: (0, 0))] * 2
        + [pl.BlockSpec((features, step), lambda i: (0, i))]
        + [pl.BlockSpec(memory_space=pl.ANY)] * len(before),
        out_specs=pl.BlockSpec((2, step), lambda i: (0, i)),
        out_shape=jax.ShapeDtypeStruct((2, units), jnp.float32),
        cost_estimate=pl.CostEstimate(
            flops=32 * features * units, bytes_accessed=2 * features * units, transcendentals=0
        ),
    )(gain.reshape(1, features), bias.reshape(1, features), weight, *before)


def second_kernel(*refs):
    tiles, weight, out, total = refs[:-3], refs[-3], refs[-2], refs[-1]
    rows = out.shape[1]
    left = jnp.concatenate([tile[...] for tile in tiles])
    value = jnp.dot(left, weight[...], preferred_element_type=jnp.float32)

    @pl.when(pl.program_id(0) == 0)
    def _():
        total[...] = value

    @pl.when(pl.program_id(0) > 0)
    def _():
        total[...] += value

    @pl.when(pl.program_id(0) == pl.num_programs(0) - 1)
    def _():
        for slot in range(out.shape[0]):
            out[slot] = total[slot * rows : (slot + 1) * rows].astype(jnp.bfloat16)


def second_product(tiles, weight, rows):
    units, features = weight.shape
    step = 512
    tokens = sum(tile.shape[0] for tile in tiles)
    return pl.pallas_call(
        second_kernel,
        grid=(units // step,),
        in_specs=[pl.BlockSpec((tile.shape[0], step), lambda i: (0, i)) for tile in tiles]
        + [pl.BlockSpec((step, features), lambda i: (i, 0))],
        out_specs=pl.BlockSpec((tokens // rows, rows, features), lambda i: (0, 0, 0)),
        out_shape=jax.ShapeDtypeStruct((tokens // rows, rows, features), jnp.bfloat16),
        scratch_shapes=[pltpu.VMEM((tokens, features), jnp.float32)],
        compiler_params=pltpu.CompilerParams(vmem_limit_bytes=24 * megabyte),
        cost_estimate=pl.CostEstimate(
            flops=2 * tokens * features * units,
            bytes_accessed=2 * (features * units + tokens * (features + units)),
            transcendentals=0,
        ),
    )(*tiles, weight)


def last_kernel(place, *refs):
    tiles, weight, done, out, total = refs[:4], refs[4], refs[5:7], refs[7], refs[8]
    rows = tiles[0].shape[0]
    left = jnp.concatenate([tile[...] for tile in tiles])
    value = jnp.dot(left, weight[...], preferred_element_type=jnp.float32)
    numbers = near_and_far(place[0], place[1])
    ends = (numbers[8], numbers[15])
    others = numbers[:8] + numbers[9:15]

    @pl.when(pl.program_id(0) == 0)
    def _():
        total[...] = value
        for part in range(parts):
            for slot, number in enumerate(others):
                out[number, part * rows : (part + 1) * rows] = done[part][slot]

    @pl.when(pl.program_id(0) > 0)
    def _():
        total[...] += value

    @pl.when(pl.program_id(0) == pl.num_programs(0) - 1)
    def _():
        for part in range(parts):
            for slot, number in enumerate(ends):
                first = (2 * part + slot) * rows
                out[number, part * rows : (part + 1) * rows] = total[first : first + rows].astype(
                    jnp.bfloat16
                )


def last_product(place, tiles, weight, done):
    units, features = weight.shape
    rows, step = tiles[0].shape[0], 1024
    shape = (16, parts * rows, features)
    return pl.pallas_call(
        last_kernel,
        grid=(units // step,),
        in_specs=[pl.BlockSpec(memory_space=pltpu.SMEM)]
        + [pl.BlockSpec((rows, step), lambda i: (0, i)) for tile in tiles]
        + [pl.BlockSpec((step, features), lambda i: (i, 0))]
        + [pl.BlockSpec(value.shape, lambda i: (0, 0, 0)) for value in done],
        out_specs=pl.BlockSpec(shape, lambda i: (0, 0, 0)),
        out_shape=jax.ShapeDtypeStruct(shape, jnp.bfloat16),
        scratch_shapes=[pltpu.VMEM((len(tiles) * rows, features), jnp.float32)],
        compiler_params=pltpu.CompilerParams(vmem_limit_bytes=24 * megabyte),
        cost_estimate=pl.CostEstimate(
            flops=2 * len(tiles) * rows * features * units,
            bytes_accessed=2 * features * (units + 32 * parts * rows),
            transcendentals=0,
        ),
    )(place, *tiles, weight, *done)


def body(tokens, norm_gain, norm_bias, weight_in, bias_in, weight_out, bias_out):
    core, z = lax.axis_index("core"), lax.axis_index("z")
    place = jnp.stack([z, core]).astype(jnp.int32)
    rows = tokens.shape[0] // parts
    ready = jnp.broadcast_to(tokens[None], (16,) + tokens.shape)
    gathered = lax.all_to_all(ready, plane, 0, 0, tiled=True)
    tops = gather_tops(tops_product(norm_gain, norm_bias, weight_in, ready))

    def tile(value, number):
        return value[rows * (2 * number - 1) : rows * (2 * number + 1)]

    def spread(hidden):
        moving = jnp.concatenate([hidden, swap(hidden)])
        own, other = [moving], []
        for number in (1, 2, 3, 4):
            moving = onward(moving if number < 4 else moving[:rows])
            own.append(moving)
            other.append(swap(moving))
        return own + other

    before, hiddens = tops[2], []
    for part in range(parts):
        theirs, ours = first_product(place, gathered, part, norm_gain, weight_in, before)
        before = theirs
        theirs = swap(theirs)
        moving = onward(low(ours[:rows], theirs[:rows]))
        moving = jnp.concatenate([moving, jnp.zeros_like(moving)])
        for number in (1, 2, 3):
            moving = onward(low(tile(ours, number), tile(theirs, number), moving))
        other = swap(low(ours[8 * rows :], moving[rows:]))
        hiddens.append(activate(place, ours, moving, other, tops, bias_in))
    done, last = [], []
    for hidden in hiddens:
        tiles = spread(hidden)
        done.append(second_product(tiles[:4] + tiles[5:8], weight_out, rows))
        last += [tiles[4], tiles[8]]
    shares = last_product(place, last, weight_out, done)
    arrived = lax.all_to_all(shares, plane, 0, 0, tiled=True)
    return (add(jnp.sum(arrived.astype(jnp.float32), axis=0), tokens) + bias_out).astype(
        jnp.bfloat16
    )


def solution(mesh):
    fine = Mesh(mesh.devices.reshape(8, 2, 4, 4), ("z", "core", "y", "x"))
    row, col = ("z", "core"), ("y", "x")
    placed = (P(col, row), P(row), P(row), P(row, col), P(col), P(col, row), P(row))
    return jax.shard_map(
        body, mesh=fine, in_specs=placed, out_specs=P(col, row), check_vma=False
    )
```

time: 326 us -> 177 us (0.54)
  waiting for transfers between devices: 233 us -> 30.6 us
  starting transfers between devices: 0.13 us -> 76.3 us
  Pallas kernels: 0 us -> 31.3 us
  blocking collectives: 53.2 us -> 28.5 us
  matrix products: 18.4 us -> 0 us
  between operations: 13.2 us -> 0.26 us
  local copies, waits for them, and re-layouts: 0.02 us -> 6.47 us
  other arithmetic: 7.37 us -> 3.04 us
    reduce_scatter x2 -> x0, waiting for transfers between devices: 139 us -> none  [the longest x1 75.4 us: body(): lax.psum_scatter(partial_value.astype(jnp.bfloat16), 'col', scatter_dimen...]
    all_gather x2 -> x0, waiting for transfers between devices: 94.1 us -> none  [the longest x1 48.3 us: body(): lax.all_gather(hidden, 'row', axis=0, tiled=True)]
    ppermute x0 -> x36, starting transfers between devices: none -> 68.6 us  [the longest x20 40.2 us: onward(): return lax.ppermute(value, ('z', 'core'), pairs)]
    psum x2 -> x0, blocking collectives: 53.2 us -> none  [the longest x1 27.4 us: body(): sums_one = lax.psum(jnp.sum(floats, axis=1), 'row')]
    pallas_call x0 -> x8, Pallas kernels: none -> 31.3 us  [the longest x2 12.3 us: first_product(): pl.pallas_call(first_kernel, grid=((units + 128) // step,), in_specs=[pl....]
    ppermute x0 -> x36, waiting for transfers between devices: none -> 30.6 us  [the longest x20 27 us: onward(): return lax.ppermute(value, ('z', 'core'), pairs)]
    all_to_all x0 -> x1, blocking collectives: none -> 28.5 us  [body(): arrived = lax.all_to_all(shares, plane, 0, 0, tiled=True)]
    dot_general x2 -> x0, matrix products: 18.4 us -> none  [the longest x1 9.38 us: body(): jnp.dot(lax.all_gather(hidden, 'row', axis=0, tiled=True), weight_out, pr...]
  transfers between devices with their start and end apart: 4 -> 37, of which waited for: 4 -> 17; matrix products, arithmetic and copies ran while one was open for 0% -> 2% of each run, Pallas kernels for 0% -> 13%
where the time goes in v1:
time: 177 us
  starting transfers between devices  76.3 us (43%)
  Pallas kernels  31.3 us (18%)
  waiting for transfers between devices  30.6 us (17%)
  blocking collectives  28.5 us (16%)
  local copies, waits for them, and re-layouts  6.47 us (4%)
  other arithmetic  3.04 us (2%)
    ppermute x20, starting transfers between devices, onward(): return lax.ppermute(value, ('z', 'core'), pairs)  40.2 us
    all_to_all x1, blocking collectives, body(): arrived = lax.all_to_all(shares, plane, 0, 0, tiled=True)  28.5 us
    ppermute x16, starting transfers between devices, swap(): return lax.ppermute(value, 'core', [(0, 1), (1, 0)])  28.4 us
    ppermute x20, waiting for transfers between devices, onward(): return lax.ppermute(value, ('z', 'core'), pairs)  27 us
    pallas_call x2, Pallas kernels, first_product(): pl.pallas_call(first_kernel, grid=((units + 128) // step,), in_specs=[pl....  12.3 us
    pallas_call x2, Pallas kernels, second_product(): pl.pallas_call(second_kernel, grid=(units // step,), in_specs=[pl.BlockSp...  8.57 us
    all_to_all x1, starting transfers between devices, body(): gathered = lax.all_to_all(ready, plane, 0, 0, tiled=True)  7.72 us
    pallas_call x1, Pallas kernels, tops_product(): pl.pallas_call(tops_kernel, grid=(units // step,), in_specs=[pl.BlockSpec...  5.42 us
  transfers between devices with their start and end apart: 37, of which 17 were waited for; matrix products, arithmetic and copies ran while one was open for 2% of the time, Pallas kernels for 13%

profile of v1, /device:TPU:1, one launch (start us, length us, event | category | flops | bytes accessed | tf_op | source)
XLA Modules:
  0.0 176.6 jit_solution(15163575473258255492)
XLA Ops:
  0.0 2.2 %broadcast_in_dim.4.refs_0_ = bf16[16,64,768]{2,1,0:T(8,128)(2,1)} broadcast(bf16[64,768]{1,0:T(8,128)(2,1)} %param.7), dimensions={1,2} | broadcast | bytes 1671168 | tf_op jit(solution)/shard_map/broadcast_in_dim | solution.py:327
  2.2 7.7 %all-to-all-start = ((bf16[16,64,768]{2,1,0:T(8,128)(2,1)}), bf16[16,64,768]{2,1,0:T(8,128)(2,1)S(1)}, u32[]{:S(2)}, u32[]{:S(2)}) async-start(bf16[16,64,768]{2,1,0:T(8,128)(2,1)} %broadcast_in_dim.4.refs_0_), calls=%async_computation | async-start | bytes 3145728 | tf_op jit(solution)/shard_map/all_to_all | solution.py:328
  11.1 5.4 %shard_map.73 = f32[2,3072]{1,0:T(2,128)} custom-call(f32[1,768]{1,0:T(1,128)} %reshape.14.gain, f32[1,768]{1,0:T(1,128)} %reshape.15.bias, bf16[768,3072]{1,0:T(8,128)(2,1)} %weight.5, bf16[16,64,768]{2,1,0:T(8,128)(2,1)} %broadcast_in_dim.4.refs_0_), custom_call_target="tpu_custom_call" | custom-call | flops 75497472 | bytes 4718592 | tf_op jit(solution)/shard_map/pallas_call | solution.py:215
  19.4 6.5 %collective-permute-start.3 = (f32[2,2,3072]{2,1,0:T(2,128)S(1)}, f32[2,2,3072]{2,1,0:T(2,128)S(1)}, u32[]{:S(2)}, u32[]{:S(2)}) collective-permute-start(f32[2,2,3072]{2,1,0:T(2,128)S(1)} %pad_maximum_fusion.3.pair), channel_id=1, source_target_pairs={{0,96},{16,176},{32,128},{48,208},{64,160},{80,240},{96,192},{112,... | collective-permute-start | bytes 147464 | tf_op jit(solution)/shard_map/ppermute | solution.py:25
  26.6 4.5 %collective-permute-start.4 = (f32[2,3072]{1,0:T(2,128)}, f32[2,3072]{1,0:T(2,128)S(1)}, u32[]{:S(2)}, u32[]{:S(2)}) collective-permute-start(f32[2,3072]{1,0:T(2,128)} %shard_map.73), channel_id=1, source_target_pairs={{0,128},{16,144},{32,160},{48,176},{64,192},{80,208},{96,224},{112... | collective-permute-start | bytes 73736 | tf_op jit(solution)/shard_map/ppermute | solution.py:25
  31.1 2.9 %collective-permute-done.4 = f32[2,3072]{1,0:T(2,128)S(1)} collective-permute-done((f32[2,3072]{1,0:T(2,128)}, f32[2,3072]{1,0:T(2,128)S(1)}, u32[]{:S(2)}, u32[]{:S(2)}) %collective-permute-start.4) | collective-permute-done | bytes 24608 | tf_op jit(solution)/shard_map/ppermute | solution.py:25
  34.1 3.1 %collective-permute-start.5 = (f32[7,2,3072]{2,1,0:T(2,128)S(1)}, f32[7,2,3072]{2,1,0:T(2,128)S(1)}, u32[]{:S(2)}, u32[]{:S(2)}) collective-permute-start(f32[7,2,3072]{2,1,0:T(2,128)S(1)} %pad_maximum_fusion.2.near), channel_id=1, source_target_pairs={{0,16},{16,0},{1,17},{17,1},{2,18},{18,2},{3,19},{19,3},{4,20},{20... | collective-permute-start | bytes 516104 | tf_op jit(solution)/shard_map/ppermute | solution.py:17
  38.2 2.3 %copy-done = bf16[768,3072]{1,0:T(8,128)(2,1)S(1)} copy-done((bf16[768,3072]{1,0:T(8,128)(2,1)S(1)}, bf16[768,3072]{1,0:T(8,128)(2,1)}, u32[]{:S(2)}) %copy-start) | copy-done | bytes 4718616
  40.5 6.2 %shard_map.74 = (bf16[224,3200]{1,0:T(8,128)(2,1)S(1)}, bf16[288,3200]{1,0:T(8,128)(2,1)S(1)}) custom-call(s32[2]{0:T(128)S(1)} %pad_add_fusion.place, bf16[16,64,768]{2,1,0:T(8,128)(2,1)S(1)} %all-to-all-done.gathered, f32[1,768]{1,0:T(1,128)S(1)} %copy-done.2, bf16[768,3072]{1,0:T(8,128)(2,1)S(1)} %copy-done, ...), custom_call_target="tpu_custom_call" | custom-call | flops 2415919104 | bytes 8650752 | tf_op jit(solution)/shard_map/pallas_call | solution.py:112
  47.1 6.2 %shard_map.76 = (bf16[224,3200]{1,0:T(8,128)(2,1)S(1)}, bf16[288,3200]{1,0:T(8,128)(2,1)S(1)}) custom-call(s32[2]{0:T(128)S(1)} %pad_add_fusion.place, bf16[16,64,768]{2,1,0:T(8,128)(2,1)S(1)} %all-to-all-done.gathered, f32[1,768]{1,0:T(1,128)S(1)} %copy-done.2, bf16[768,3072]{1,0:T(8,128)(2,1)S(1)} %copy-done, bf16[224,3200]{1,0:T(8,128)(2,1)S(1)} %get-tuple-element.10.refs_0_), custom_call_target="tpu_custom_call" | custom-call | flops 2415919104 | bytes 8650752 | tf_op jit(solution)/shard_map/pallas_call | solution.py:112
  53.6 2.4 %collective-permute-start.7 = (bf16[32,3200]{1,0:T(8,128)(2,1)S(1)}, bf16[32,3200]{1,0:T(8,128)(2,1)S(1)}, u32[]{:S(2)}, u32[]{:S(2)}) collective-permute-start(bf16[32,3200]{1,0:T(8,128)(2,1)S(1)} %add_convert_fusion.9), channel_id=1, source_target_pairs={{0,32},{16,240},{32,64},{48,16},{64,96},{80,48},{96,128},{112,80},... | collective-permute-start | bytes 614408 | tf_op jit(solution)/shard_map/ppermute | solution.py:25
  56.7 2.5 %collective-permute-start.19 = (bf16[32,3200]{1,0:T(8,128)(2,1)S(1)}, bf16[32,3200]{1,0:T(8,128)(2,1)S(1)}, u32[]{:S(2)}, u32[]{:S(2)}) collective-permute-start(bf16[32,3200]{1,0:T(8,128)(2,1)S(1)} %add_convert_fusion.7), channel_id=1, source_target_pairs={{0,32},{16,240},{32,64},{48,16},{64,96},{80,48},{96,128},{112,80},... | collective-permute-start | bytes 614408 | tf_op jit(solution)/shard_map/ppermute | solution.py:25
  59.3 2.7 %collective-permute-start.8 = (bf16[64,3200]{1,0:T(8,128)(2,1)S(1)}, bf16[64,3200]{1,0:T(8,128)(2,1)S(1)}, u32[]{:S(2)}, u32[]{:S(2)}) collective-permute-start(bf16[64,3200]{1,0:T(8,128)(2,1)S(1)} %add_convert_fusion.5), channel_id=1, source_target_pairs={{0,32},{16,240},{32,64},{48,16},{64,96},{80,48},{96,128},{112,80},... | collective-permute-start | bytes 1228808 | tf_op jit(solution)/shard_map/ppermute | solution.py:25
  62.2 3.2 %collective-permute-start.20 = (bf16[64,3200]{1,0:T(8,128)(2,1)S(1)}, bf16[64,3200]{1,0:T(8,128)(2,1)S(1)}, u32[]{:S(2)}, u32[]{:S(2)}) collective-permute-start(bf16[64,3200]{1,0:T(8,128)(2,1)S(1)} %add_convert_fusion.2), channel_id=1, source_target_pairs={{0,32},{16,240},{32,64},{48,16},{64,96},{80,48},{96,128},{112,80},... | collective-permute-start | bytes 1228808 | tf_op jit(solution)/shard_map/ppermute | solution.py:25
  67.1 3.2 %collective-permute-start.9 = (bf16[64,3200]{1,0:T(8,128)(2,1)S(1)}, bf16[64,3200]{1,0:T(8,128)(2,1)S(1)}, u32[]{:S(2)}, u32[]{:S(2)}) collective-permute-start(bf16[64,3200]{1,0:T(8,128)(2,1)S(1)} %add_convert_fusion.4), channel_id=1, source_target_pairs={{0,32},{16,240},{32,64},{48,16},{64,96},{80,48},{96,128},{112,80},... | collective-permute-start | bytes 1228808 | tf_op jit(solution)/shard_map/ppermute | solution.py:25
  71.5 3.2 %collective-permute-start.21 = (bf16[64,3200]{1,0:T(8,128)(2,1)S(1)}, bf16[64,3200]{1,0:T(8,128)(2,1)S(1)}, u32[]{:S(2)}, u32[]{:S(2)}) collective-permute-start(bf16[64,3200]{1,0:T(8,128)(2,1)S(1)} %add_convert_fusion.1), channel_id=1, source_target_pairs={{0,32},{16,240},{32,64},{48,16},{64,96},{80,48},{96,128},{112,80},... | collective-permute-start | bytes 1228808 | tf_op jit(solution)/shard_map/ppermute | solution.py:25
  75.9 3.2 %collective-permute-start.10 = (bf16[64,3200]{1,0:T(8,128)(2,1)S(1)}, bf16[64,3200]{1,0:T(8,128)(2,1)S(1)}, u32[]{:S(2)}, u32[]{:S(2)}) collective-permute-start(bf16[64,3200]{1,0:T(8,128)(2,1)S(1)} %add_convert_fusion.3), channel_id=1, source_target_pairs={{0,32},{16,240},{32,64},{48,16},{64,96},{80,48},{96,128},{112,80},... | collective-permute-start | bytes 1228808 | tf_op jit(solution)/shard_map/ppermute | solution.py:25
  80.2 3.2 %collective-permute-start.22 = (bf16[64,3200]{1,0:T(8,128)(2,1)S(1)}, bf16[64,3200]{1,0:T(8,128)(2,1)S(1)}, u32[]{:S(2)}, u32[]{:S(2)}) collective-permute-start(bf16[64,3200]{1,0:T(8,128)(2,1)S(1)} %add_convert_fusion), channel_id=1, source_target_pairs={{0,32},{16,240},{32,64},{48,16},{64,96},{80,48},{96,128},{112,80},... | collective-permute-start | bytes 1228808 | tf_op jit(solution)/shard_map/ppermute | solution.py:25
  84.5 4.9 %collective-permute-start.11 = (bf16[32,3200]{1,0:T(8,128)(2,1)S(1)}, bf16[32,3200]{1,0:T(8,128)(2,1)S(1)}, u32[]{:S(2)}, u32[]{:S(2)}) collective-permute-start(bf16[32,3200]{1,0:T(8,128)(2,1)S(1)} %add_convert_fusion.8), channel_id=1, source_target_pairs={{0,16},{16,0},{1,17},{17,1},{2,18},{18,2},{3,19},{19,3},{4,20},{20... | collective-permute-start | bytes 614408 | tf_op jit(solution)/shard_map/ppermute | solution.py:17
  89.5 4.3 %collective-permute-start.23 = (bf16[32,3200]{1,0:T(8,128)(2,1)S(1)}, bf16[32,3200]{1,0:T(8,128)(2,1)S(1)}, u32[]{:S(2)}, u32[]{:S(2)}) collective-permute-start(bf16[32,3200]{1,0:T(8,128)(2,1)S(1)} %add_convert_fusion.6), channel_id=1, source_target_pairs={{0,16},{16,0},{1,17},{17,1},{2,18},{18,2},{3,19},{19,3},{4,20},{20... | collective-permute-start | bytes 614408 | tf_op jit(solution)/shard_map/ppermute | solution.py:17
  98.6 5.8 %collective-permute-done.13.refs_1_ = bf16[64,3072]{1,0:T(8,128)(2,1)S(1)} collective-permute-done((bf16[64,3072]{1,0:T(8,128)(2,1)S(1)}, bf16[64,3072]{1,0:T(8,128)(2,1)S(1)}, u32[]{:S(2)}, u32[]{:S(2)}) %collective-permute-start.13) | collective-permute-done | bytes 393248 | tf_op jit(solution)/shard_map/ppermute | solution.py:25
  105.4 3.3 %collective-permute-done.25.refs_1_ = bf16[64,3072]{1,0:T(8,128)(2,1)S(1)} collective-permute-done((bf16[64,3072]{1,0:T(8,128)(2,1)S(1)}, bf16[64,3072]{1,0:T(8,128)(2,1)S(1)}, u32[]{:S(2)}, u32[]{:S(2)}) %collective-permute-start.25) | collective-permute-done | bytes 393248 | tf_op jit(solution)/shard_map/ppermute | solution.py:25
  109.6 3.3 %collective-permute-done.14.refs_2_ = bf16[64,3072]{1,0:T(8,128)(2,1)S(1)} collective-permute-done((bf16[64,3072]{1,0:T(8,128)(2,1)S(1)}, bf16[64,3072]{1,0:T(8,128)(2,1)S(1)}, u32[]{:S(2)}, u32[]{:S(2)}) %collective-permute-start.14) | collective-permute-done | bytes 393248 | tf_op jit(solution)/shard_map/ppermute | solution.py:25
  113.8 3.3 %collective-permute-done.26.refs_2_ = bf16[64,3072]{1,0:T(8,128)(2,1)S(1)} collective-permute-done((bf16[64,3072]{1,0:T(8,128)(2,1)S(1)}, bf16[64,3072]{1,0:T(8,128)(2,1)S(1)}, u32[]{:S(2)}, u32[]{:S(2)}) %collective-permute-start.26) | collective-permute-done | bytes 393248 | tf_op jit(solution)/shard_map/ppermute | solution.py:25
  121.3 3.2 %collective-permute-start.32 = (bf16[64,3072]{1,0:T(8,128)(2,1)S(1)}, bf16[64,3072]{1,0:T(8,128)(2,1)S(1)}, u32[]{:S(2)}, u32[]{:S(2)}) collective-permute-start(bf16[64,3072]{1,0:T(8,128)(2,1)S(1)} %collective-permute-done.15.refs_3_), channel_id=1, source_target_pairs={{0,16},{16,0},{1,17},{17,1},{2,18},{18,2},{3,19},{19,3},{4,20},{20... | collective-permute-start | bytes 1179656 | tf_op jit(solution)/shard_map/ppermute | solution.py:17
  126.5 2.4 %collective-permute-start.33 = (bf16[64,3072]{1,0:T(8,128)(2,1)S(1)}, bf16[64,3072]{1,0:T(8,128)(2,1)S(1)}, u32[]{:S(2)}, u32[]{:S(2)}) collective-permute-start(bf16[64,3072]{1,0:T(8,128)(2,1)S(1)} %collective-permute-done.25.refs_1_), channel_id=1, source_target_pairs={{0,16},{16,0},{1,17},{17,1},{2,18},{18,2},{3,19},{19,3},{4,20},{20... | collective-permute-start | bytes 1179656 | tf_op jit(solution)/shard_map/ppermute | solution.py:17
  129.4 2.1 %collective-permute-start.35 = (bf16[64,3072]{1,0:T(8,128)(2,1)S(1)}, bf16[64,3072]{1,0:T(8,128)(2,1)S(1)}, u32[]{:S(2)}, u32[]{:S(2)}) collective-permute-start(bf16[64,3072]{1,0:T(8,128)(2,1)S(1)} %collective-permute-done.27.refs_3_), channel_id=1, source_target_pairs={{0,16},{16,0},{1,17},{17,1},{2,18},{18,2},{3,19},{19,3},{4,20},{20... | collective-permute-start | bytes 1179656 | tf_op jit(solution)/shard_map/ppermute | solution.py:17
  131.5 4.2 %collective-permute-start.17 = (bf16[32,3072]{1,0:T(8,128)(2,1)S(1)}, bf16[32,3072]{1,0:T(8,128)(2,1)S(1)}, u32[]{:S(2)}, u32[]{:S(2)}) collective-permute-start(bf16[32,3072]{1,0:T(8,128)(2,1)S(1)} %collective-permute-done.16.refs_0_), channel_id=1, source_target_pairs={{0,16},{16,0},{1,17},{17,1},{2,18},{18,2},{3,19},{19,3},{4,20},{20... | collective-permute-start | bytes 589832 | tf_op jit(solution)/shard_map/ppermute | solution.py:17
  135.8 4.3 %shard_map.78.refs_5_ = bf16[14,32,768]{2,1,0:T(8,128)(2,1)S(1)} custom-call(bf16[64,3072]{1,0:T(8,128)(2,1)S(1)} %pad_maximum_fusion.refs_0_, bf16[64,3072]{1,0:T(8,128)(2,1)S(1)} %collective-permute-done.13.refs_1_, bf16[64,3072]{1,0:T(8,128)(2,1)S(1)} %collective-permute-done.14.refs_2_, bf16[64,3072]{1,0:T(8,128)(2,1)S(1)} %collective-permute-done.15.refs_3_, ...), custom_call_target="tpu_custom_call" | custom-call | flops 2113929216 | bytes 8159232 | tf_op jit(solution)/shard_map/pallas_call | solution.py:253
  140.1 4.3 %shard_map.79.refs_6_ = bf16[14,32,768]{2,1,0:T(8,128)(2,1)S(1)} custom-call(bf16[64,3072]{1,0:T(8,128)(2,1)S(1)} %pad_maximum_fusion.1.refs_0_, bf16[64,3072]{1,0:T(8,128)(2,1)S(1)} %collective-permute-done.25.refs_1_, bf16[64,3072]{1,0:T(8,128)(2,1)S(1)} %collective-permute-done.26.refs_2_, bf16[64,3072]{1,0:T(8,128)(2,1)S(1)} %collective-permute-done.27.refs_3_, ...), custom_call_target="tpu_custom_call" | custom-call | flops 2113929216 | bytes 8159232 | tf_op jit(solution)/shard_map/pallas_call | solution.py:253
  144.4 2.1 %shard_map.80 = bf16[16,64,768]{2,1,0:T(8,128)(2,1)S(1)} custom-call(s32[2]{0:T(128)S(1)} %pad_add_fusion.place, bf16[32,3072]{1,0:T(8,128)(2,1)S(1)} %collective-permute-done.16.refs_0_, bf16[32,3072]{1,0:T(8,128)(2,1)S(1)} %collective-permute-done.17.refs_1_, bf16[32,3072]{1,0:T(8,128)(2,1)S(1)} %collective-permute-done.28.refs_2_, ...), custom_call_target="tpu_custom_call" | custom-call | flops 603979776 | bytes 7864320 | tf_op jit(solution)/shard_map/pallas_call | solution.py:304
  146.5 28.5 %all_to_all.10 = bf16[16,64,768]{2,1,0:T(8,128)(2,1)S(1)} all-to-all(bf16[16,64,768]{2,1,0:T(8,128)(2,1)S(1)} %shard_map.80), channel_id=1, replica_groups=mesh['z'=8,'core'=2,'y'=4,'x'=4] {'y','x'}, dimensions={0} | all-to-all | bytes 3145728 | tf_op jit(solution)/shard_map/all_to_all | solution.py:360
  (92 shorter events, 29.8 us)
Async XLA Ops:
  2.2 36.0 %all-to-all-start = ((bf16[16,64,768]{2,1,0:T(8,128)(2,1)}), bf16[16,64,768]{2,1,0:T(8,128)(2,1)S(1)}, u32[]{:S(2)}, u32[]{:S(2)}) async-start(bf16[16,64,768]{2,1,0:T(8,128)(2,1)} %broadcast_in_dim.4.refs_0_), calls=%async_computation | async-start | bytes 3145728 | tf_op jit(solution)/shard_map/all_to_all | solution.py:328
  19.4 14.6 %collective-permute-start.3 = (f32[2,2,3072]{2,1,0:T(2,128)S(1)}, f32[2,2,3072]{2,1,0:T(2,128)S(1)}, u32[]{:S(2)}, u32[]{:S(2)}) collective-permute-start(f32[2,2,3072]{2,1,0:T(2,128)S(1)} %pad_maximum_fusion.3.pair), channel_id=1, source_target_pairs={{0,96},{16,176},{32,128},{48,208},{64,160},{80,240},{96,192},{112,... | collective-permute-start | bytes 147464 | tf_op jit(solution)/shard_map/ppermute | solution.py:25
  25.9 8.1 %collective-permute-start.2 = (f32[2,2,3072]{2,1,0:T(2,128)S(1)}, f32[2,2,3072]{2,1,0:T(2,128)S(1)}, u32[]{:S(2)}, u32[]{:S(2)}) collective-permute-start(f32[2,2,3072]{2,1,0:T(2,128)S(1)} %pad_maximum_fusion.3.pair), channel_id=1, source_target_pairs={{0,64},{16,208},{32,96},{48,240},{64,128},{80,16},{96,160},{112,48... | collective-permute-start | bytes 147464 | tf_op jit(solution)/shard_map/ppermute | solution.py:25
  26.2 7.8 %collective-permute-start.1 = (f32[2,2,3072]{2,1,0:T(2,128)S(1)}, f32[2,2,3072]{2,1,0:T(2,128)S(1)}, u32[]{:S(2)}, u32[]{:S(2)}) collective-permute-start(f32[2,2,3072]{2,1,0:T(2,128)S(1)} %pad_maximum_fusion.3.pair), channel_id=1, source_target_pairs={{0,32},{16,240},{32,64},{48,16},{64,96},{80,48},{96,128},{112,80},... | collective-permute-start | bytes 147464 | tf_op jit(solution)/shard_map/ppermute | solution.py:25
  26.6 7.4 %collective-permute-start.4 = (f32[2,3072]{1,0:T(2,128)}, f32[2,3072]{1,0:T(2,128)S(1)}, u32[]{:S(2)}, u32[]{:S(2)}) collective-permute-start(f32[2,3072]{1,0:T(2,128)} %shard_map.73), channel_id=1, source_target_pairs={{0,128},{16,144},{32,160},{48,176},{64,192},{80,208},{96,224},{112... | collective-permute-start | bytes 73736 | tf_op jit(solution)/shard_map/ppermute | solution.py:25
  46.7 6.9 %collective-permute-start.6 = (bf16[224,3200]{1,0:T(8,128)(2,1)S(1)}, bf16[224,3200]{1,0:T(8,128)(2,1)S(1)}, u32[]{:S(2)}, u32[]{:S(2)}) collective-permute-start(bf16[224,3200]{1,0:T(8,128)(2,1)S(1)} %get-tuple-element.10.refs_0_), channel_id=1, source_target_pairs={{0,16},{16,0},{1,17},{17,1},{2,18},{18,2},{3,19},{19,3},{4,20},{20... | collective-permute-start | bytes 4300808 | tf_op jit(solution)/shard_map/ppermute | solution.py:17
  53.6 5.5 %collective-permute-start.7 = (bf16[32,3200]{1,0:T(8,128)(2,1)S(1)}, bf16[32,3200]{1,0:T(8,128)(2,1)S(1)}, u32[]{:S(2)}, u32[]{:S(2)}) collective-permute-start(bf16[32,3200]{1,0:T(8,128)(2,1)S(1)} %add_convert_fusion.9), channel_id=1, source_target_pairs={{0,32},{16,240},{32,64},{48,16},{64,96},{80,48},{96,128},{112,80},... | collective-permute-start | bytes 614408 | tf_op jit(solution)/shard_map/ppermute | solution.py:25
  56.7 5.4 %collective-permute-start.19 = (bf16[32,3200]{1,0:T(8,128)(2,1)S(1)}, bf16[32,3200]{1,0:T(8,128)(2,1)S(1)}, u32[]{:S(2)}, u32[]{:S(2)}) collective-permute-start(bf16[32,3200]{1,0:T(8,128)(2,1)S(1)} %add_convert_fusion.7), channel_id=1, source_target_pairs={{0,32},{16,240},{32,64},{48,16},{64,96},{80,48},{96,128},{112,80},... | collective-permute-start | bytes 614408 | tf_op jit(solution)/shard_map/ppermute | solution.py:25
  59.3 7.6 %collective-permute-start.8 = (bf16[64,3200]{1,0:T(8,128)(2,1)S(1)}, bf16[64,3200]{1,0:T(8,128)(2,1)S(1)}, u32[]{:S(2)}, u32[]{:S(2)}) collective-permute-start(bf16[64,3200]{1,0:T(8,128)(2,1)S(1)} %add_convert_fusion.5), channel_id=1, source_target_pairs={{0,32},{16,240},{32,64},{48,16},{64,96},{80,48},{96,128},{112,80},... | collective-permute-start | bytes 1228808 | tf_op jit(solution)/shard_map/ppermute | solution.py:25
  62.2 9.1 %collective-permute-start.20 = (bf16[64,3200]{1,0:T(8,128)(2,1)S(1)}, bf16[64,3200]{1,0:T(8,128)(2,1)S(1)}, u32[]{:S(2)}, u32[]{:S(2)}) collective-permute-start(bf16[64,3200]{1,0:T(8,128)(2,1)S(1)} %add_convert_fusion.2), channel_id=1, source_target_pairs={{0,32},{16,240},{32,64},{48,16},{64,96},{80,48},{96,128},{112,80},... | collective-permute-start | bytes 1228808 | tf_op jit(solution)/shard_map/ppermute | solution.py:25
  67.1 8.6 %collective-permute-start.9 = (bf16[64,3200]{1,0:T(8,128)(2,1)S(1)}, bf16[64,3200]{1,0:T(8,128)(2,1)S(1)}, u32[]{:S(2)}, u32[]{:S(2)}) collective-permute-start(bf16[64,3200]{1,0:T(8,128)(2,1)S(1)} %add_convert_fusion.4), channel_id=1, source_target_pairs={{0,32},{16,240},{32,64},{48,16},{64,96},{80,48},{96,128},{112,80},... | collective-permute-start | bytes 1228808 | tf_op jit(solution)/shard_map/ppermute | solution.py:25
  71.5 8.6 %collective-permute-start.21 = (bf16[64,3200]{1,0:T(8,128)(2,1)S(1)}, bf16[64,3200]{1,0:T(8,128)(2,1)S(1)}, u32[]{:S(2)}, u32[]{:S(2)}) collective-permute-start(bf16[64,3200]{1,0:T(8,128)(2,1)S(1)} %add_convert_fusion.1), channel_id=1, source_target_pairs={{0,32},{16,240},{32,64},{48,16},{64,96},{80,48},{96,128},{112,80},... | collective-permute-start | bytes 1228808 | tf_op jit(solution)/shard_map/ppermute | solution.py:25
  75.9 8.6 %collective-permute-start.10 = (bf16[64,3200]{1,0:T(8,128)(2,1)S(1)}, bf16[64,3200]{1,0:T(8,128)(2,1)S(1)}, u32[]{:S(2)}, u32[]{:S(2)}) collective-permute-start(bf16[64,3200]{1,0:T(8,128)(2,1)S(1)} %add_convert_fusion.3), channel_id=1, source_target_pairs={{0,32},{16,240},{32,64},{48,16},{64,96},{80,48},{96,128},{112,80},... | collective-permute-start | bytes 1228808 | tf_op jit(solution)/shard_map/ppermute | solution.py:25
  80.2 9.2 %collective-permute-start.22 = (bf16[64,3200]{1,0:T(8,128)(2,1)S(1)}, bf16[64,3200]{1,0:T(8,128)(2,1)S(1)}, u32[]{:S(2)}, u32[]{:S(2)}) collective-permute-start(bf16[64,3200]{1,0:T(8,128)(2,1)S(1)} %add_convert_fusion), channel_id=1, source_target_pairs={{0,32},{16,240},{32,64},{48,16},{64,96},{80,48},{96,128},{112,80},... | collective-permute-start | bytes 1228808 | tf_op jit(solution)/shard_map/ppermute | solution.py:25
  84.5 9.3 %collective-permute-start.11 = (bf16[32,3200]{1,0:T(8,128)(2,1)S(1)}, bf16[32,3200]{1,0:T(8,128)(2,1)S(1)}, u32[]{:S(2)}, u32[]{:S(2)}) collective-permute-start(bf16[32,3200]{1,0:T(8,128)(2,1)S(1)} %add_convert_fusion.8), channel_id=1, source_target_pairs={{0,16},{16,0},{1,17},{17,1},{2,18},{18,2},{3,19},{19,3},{4,20},{20... | collective-permute-start | bytes 614408 | tf_op jit(solution)/shard_map/ppermute | solution.py:17
  89.5 5.9 %collective-permute-start.23 = (bf16[32,3200]{1,0:T(8,128)(2,1)S(1)}, bf16[32,3200]{1,0:T(8,128)(2,1)S(1)}, u32[]{:S(2)}, u32[]{:S(2)}) collective-permute-start(bf16[32,3200]{1,0:T(8,128)(2,1)S(1)} %add_convert_fusion.6), channel_id=1, source_target_pairs={{0,16},{16,0},{1,17},{17,1},{2,18},{18,2},{3,19},{19,3},{4,20},{20... | collective-permute-start | bytes 614408 | tf_op jit(solution)/shard_map/ppermute | solution.py:17
  97.4 7.0 %collective-permute-start.13 = (bf16[64,3072]{1,0:T(8,128)(2,1)S(1)}, bf16[64,3072]{1,0:T(8,128)(2,1)S(1)}, u32[]{:S(2)}, u32[]{:S(2)}) collective-permute-start(bf16[64,3072]{1,0:T(8,128)(2,1)S(1)} %pad_maximum_fusion.refs_0_), channel_id=1, source_target_pairs={{0,32},{16,240},{32,64},{48,16},{64,96},{80,48},{96,128},{112,80},... | collective-permute-start | bytes 1179656 | tf_op jit(solution)/shard_map/ppermute | solution.py:25
  98.5 10.1 %collective-permute-start.25 = (bf16[64,3072]{1,0:T(8,128)(2,1)S(1)}, bf16[64,3072]{1,0:T(8,128)(2,1)S(1)}, u32[]{:S(2)}, u32[]{:S(2)}) collective-permute-start(bf16[64,3072]{1,0:T(8,128)(2,1)S(1)} %pad_maximum_fusion.1.refs_0_), channel_id=1, source_target_pairs={{0,32},{16,240},{32,64},{48,16},{64,96},{80,48},{96,128},{112,80},... | collective-permute-start | bytes 1179656 | tf_op jit(solution)/shard_map/ppermute | solution.py:25
  104.5 8.4 %collective-permute-start.14 = (bf16[64,3072]{1,0:T(8,128)(2,1)S(1)}, bf16[64,3072]{1,0:T(8,128)(2,1)S(1)}, u32[]{:S(2)}, u32[]{:S(2)}) collective-permute-start(bf16[64,3072]{1,0:T(8,128)(2,1)S(1)} %collective-permute-done.13.refs_1_), channel_id=1, source_target_pairs={{0,32},{16,240},{32,64},{48,16},{64,96},{80,48},{96,128},{112,80},... | collective-permute-start | bytes 1179656 | tf_op jit(solution)/shard_map/ppermute | solution.py:25
  108.7 8.4 %collective-permute-start.26 = (bf16[64,3072]{1,0:T(8,128)(2,1)S(1)}, bf16[64,3072]{1,0:T(8,128)(2,1)S(1)}, u32[]{:S(2)}, u32[]{:S(2)}) collective-permute-start(bf16[64,3072]{1,0:T(8,128)(2,1)S(1)} %collective-permute-done.25.refs_1_), channel_id=1, source_target_pairs={{0,32},{16,240},{32,64},{48,16},{64,96},{80,48},{96,128},{112,80},... | collective-permute-start | bytes 1179656 | tf_op jit(solution)/shard_map/ppermute | solution.py:25
  112.9 8.4 %collective-permute-start.15 = (bf16[64,3072]{1,0:T(8,128)(2,1)S(1)}, bf16[64,3072]{1,0:T(8,128)(2,1)S(1)}, u32[]{:S(2)}, u32[]{:S(2)}) collective-permute-start(bf16[64,3072]{1,0:T(8,128)(2,1)S(1)} %collective-permute-done.14.refs_2_), channel_id=1, source_target_pairs={{0,32},{16,240},{32,64},{48,16},{64,96},{80,48},{96,128},{112,80},... | collective-permute-start | bytes 1179656 | tf_op jit(solution)/shard_map/ppermute | solution.py:25
  117.1 8.4 %collective-permute-start.27 = (bf16[64,3072]{1,0:T(8,128)(2,1)S(1)}, bf16[64,3072]{1,0:T(8,128)(2,1)S(1)}, u32[]{:S(2)}, u32[]{:S(2)}) collective-permute-start(bf16[64,3072]{1,0:T(8,128)(2,1)S(1)} %collective-permute-done.26.refs_2_), channel_id=1, source_target_pairs={{0,32},{16,240},{32,64},{48,16},{64,96},{80,48},{96,128},{112,80},... | collective-permute-start | bytes 1179656 | tf_op jit(solution)/shard_map/ppermute | solution.py:25
  118.0 8.5 %collective-permute-start.30 = (bf16[64,3072]{1,0:T(8,128)(2,1)S(1)}, bf16[64,3072]{1,0:T(8,128)(2,1)S(1)}, u32[]{:S(2)}, u32[]{:S(2)}) collective-permute-start(bf16[64,3072]{1,0:T(8,128)(2,1)S(1)} %collective-permute-done.13.refs_1_), channel_id=1, source_target_pairs={{0,16},{16,0},{1,17},{17,1},{2,18},{18,2},{3,19},{19,3},{4,20},{20... | collective-permute-start | bytes 1179656 | tf_op jit(solution)/shard_map/ppermute | solution.py:17
  119.8 9.2 %collective-permute-start.31 = (bf16[64,3072]{1,0:T(8,128)(2,1)S(1)}, bf16[64,3072]{1,0:T(8,128)(2,1)S(1)}, u32[]{:S(2)}, u32[]{:S(2)}) collective-permute-start(bf16[64,3072]{1,0:T(8,128)(2,1)S(1)} %collective-permute-done.14.refs_2_), channel_id=1, source_target_pairs={{0,16},{16,0},{1,17},{17,1},{2,18},{18,2},{3,19},{19,3},{4,20},{20... | collective-permute-start | bytes 1179656 | tf_op jit(solution)/shard_map/ppermute | solution.py:17
  121.3 14.4 %collective-permute-start.32 = (bf16[64,3072]{1,0:T(8,128)(2,1)S(1)}, bf16[64,3072]{1,0:T(8,128)(2,1)S(1)}, u32[]{:S(2)}, u32[]{:S(2)}) collective-permute-start(bf16[64,3072]{1,0:T(8,128)(2,1)S(1)} %collective-permute-done.15.refs_3_), channel_id=1, source_target_pairs={{0,16},{16,0},{1,17},{17,1},{2,18},{18,2},{3,19},{19,3},{4,20},{20... | collective-permute-start | bytes 1179656 | tf_op jit(solution)/shard_map/ppermute | solution.py:17
  124.5 4.9 %collective-permute-start.16 = (bf16[32,3072]{1,0:T(8,128)(2,1)S(1)}, bf16[32,3072]{1,0:T(8,128)(2,1)S(1)}, u32[]{:S(2)}, u32[]{:S(2)}) collective-permute-start(bf16[32,3072]{1,0:T(8,128)(2,1)S(1)} %slice.93), channel_id=1, source_target_pairs={{0,32},{16,240},{32,64},{48,16},{64,96},{80,48},{96,128},{112,80},... | collective-permute-start | bytes 589832 | tf_op jit(solution)/shard_map/ppermute | solution.py:25
  125.5 6.0 %collective-permute-start.28 = (bf16[32,3072]{1,0:T(8,128)(2,1)S(1)}, bf16[32,3072]{1,0:T(8,128)(2,1)S(1)}, u32[]{:S(2)}, u32[]{:S(2)}) collective-permute-start(bf16[32,3072]{1,0:T(8,128)(2,1)S(1)} %slice.99), channel_id=1, source_target_pairs={{0,32},{16,240},{32,64},{48,16},{64,96},{80,48},{96,128},{112,80},... | collective-permute-start | bytes 589832 | tf_op jit(solution)/shard_map/ppermute | solution.py:25
  126.5 13.5 %collective-permute-start.33 = (bf16[64,3072]{1,0:T(8,128)(2,1)S(1)}, bf16[64,3072]{1,0:T(8,128)(2,1)S(1)}, u32[]{:S(2)}, u32[]{:S(2)}) collective-permute-start(bf16[64,3072]{1,0:T(8,128)(2,1)S(1)} %collective-permute-done.25.refs_1_), channel_id=1, source_target_pairs={{0,16},{16,0},{1,17},{17,1},{2,18},{18,2},{3,19},{19,3},{4,20},{20... | collective-permute-start | bytes 1179656 | tf_op jit(solution)/shard_map/ppermute | solution.py:17
  129.0 11.1 %collective-permute-start.34 = (bf16[64,3072]{1,0:T(8,128)(2,1)S(1)}, bf16[64,3072]{1,0:T(8,128)(2,1)S(1)}, u32[]{:S(2)}, u32[]{:S(2)}) collective-permute-start(bf16[64,3072]{1,0:T(8,128)(2,1)S(1)} %collective-permute-done.26.refs_2_), channel_id=1, source_target_pairs={{0,16},{16,0},{1,17},{17,1},{2,18},{18,2},{3,19},{19,3},{4,20},{20... | collective-permute-start | bytes 1179656 | tf_op jit(solution)/shard_map/ppermute | solution.py:17
  129.4 10.6 %collective-permute-start.35 = (bf16[64,3072]{1,0:T(8,128)(2,1)S(1)}, bf16[64,3072]{1,0:T(8,128)(2,1)S(1)}, u32[]{:S(2)}, u32[]{:S(2)}) collective-permute-start(bf16[64,3072]{1,0:T(8,128)(2,1)S(1)} %collective-permute-done.27.refs_3_), channel_id=1, source_target_pairs={{0,16},{16,0},{1,17},{17,1},{2,18},{18,2},{3,19},{19,3},{4,20},{20... | collective-permute-start | bytes 1179656 | tf_op jit(solution)/shard_map/ppermute | solution.py:17
  131.5 12.9 %collective-permute-start.17 = (bf16[32,3072]{1,0:T(8,128)(2,1)S(1)}, bf16[32,3072]{1,0:T(8,128)(2,1)S(1)}, u32[]{:S(2)}, u32[]{:S(2)}) collective-permute-start(bf16[32,3072]{1,0:T(8,128)(2,1)S(1)} %collective-permute-done.16.refs_0_), channel_id=1, source_target_pairs={{0,16},{16,0},{1,17},{17,1},{2,18},{18,2},{3,19},{19,3},{4,20},{20... | collective-permute-start | bytes 589832 | tf_op jit(solution)/shard_map/ppermute | solution.py:17
  135.7 8.7 %collective-permute-start.29 = (bf16[32,3072]{1,0:T(8,128)(2,1)S(1)}, bf16[32,3072]{1,0:T(8,128)(2,1)S(1)}, u32[]{:S(2)}, u32[]{:S(2)}) collective-permute-start(bf16[32,3072]{1,0:T(8,128)(2,1)S(1)} %collective-permute-done.28.refs_2_), channel_id=1, source_target_pairs={{0,16},{16,0},{1,17},{17,1},{2,18},{18,2},{3,19},{19,3},{4,20},{20... | collective-permute-start | bytes 589832 | tf_op jit(solution)/shard_map/ppermute | solution.py:17
  (14 other events, 175.9 us)
